TPU v7x, 1024 devices: a whole 8x8x8 slice. The times are simulated.
1024 devices in a mesh: dp: 32 (over z_lo, x), expert: 32 (over z_hi, y, core).
Axes of the slice: x: 8, y: 8, z: 8 (z_hi: 2, z_lo: 4; z = z_hi * 4 + z_lo), core: 2. Of those that a mesh axis runs over, the one named last changes fastest.
Arguments:
- tokens: bfloat16 [4096, 2048], P('expert'), may hold values from -6 to 6
- expert_ids: int32 [4096], P('expert'), may hold values from 0 to 31, as said below
- w_router: bfloat16 [2048, 32], replicated, may hold values from -0.125 to 0.125
- w_gate: bfloat16 [32, 2048, 8192], P('expert', None, 'dp'), may hold values from -0.125 to 0.125
- w_up: bfloat16 [32, 2048, 8192], P('expert', None, 'dp'), may hold values from -0.125 to 0.125
- w_down: bfloat16 [32, 8192, 2048], P('expert', 'dp'), may hold values from -0.125 to 0.125
Outputs:
- moe_out: bfloat16 [4096, 2048], P('expert', 'dp')
Inputs may be any that keep to these rules, and one draw needn't show every extreme that they name: `expert_ids`: within each block of 128 consecutive tokens no expert is named more than 12 times; one expert, the same for all blocks, is named exactly 12 times in every block.
All inputs are finite; a program needn't handle non-finite values.
Results may differ from a plain program's by a relative error of at most 0.0057.
Values may be sent and summed in bfloat16 or wider, within the bound.
A program may use at most 64 MiB of HBM per device.

v0:
```python
import jax
import jax.numpy as jnp
from jax import lax
from jax.sharding import PartitionSpec as P


def per_device(tokens, expert_ids, w_router, w_gate, w_up, w_down):
    tok_count, model_width = tokens.shape
    source_count = lax.axis_size("expert")
    local_experts = w_gate.shape[0]
    experts = local_experts * source_count
    capacity = 3 * tok_count // experts
    onehot = (expert_ids[:, None] == jnp.arange(experts, dtype=jnp.int32)[None, :]).astype(
        jnp.int32
    )
    ranking = jnp.cumsum(onehot, axis=0) - onehot
    slots = jnp.sum(ranking * onehot, axis=1)
    target = expert_ids * capacity + slots
    placing = (target[:, None] == jnp.arange(experts * capacity, dtype=jnp.int32)[None, :]).astype(
        jnp.bfloat16
    )
    outgoing = lax.dot_general(
        placing, tokens, (((0,), (0,)), ((), ())), preferred_element_type=jnp.float32
    )
    outgoing = outgoing.astype(jnp.bfloat16).reshape(
        source_count, local_experts, capacity, model_width
    )
    router = jnp.dot(tokens, w_router, preferred_element_type=jnp.float32)
    gating = jax.nn.sigmoid(jnp.sum(router * onehot.astype(jnp.float32), axis=1))
    received = lax.all_to_all(outgoing, "expert", split_axis=0, concat_axis=0, tiled=True)
    gate_pre = jnp.einsum("necd,edf->necf", received, w_gate, preferred_element_type=jnp.float32)
    lifted = jnp.einsum("necd,edf->necf", received, w_up, preferred_element_type=jnp.float32)
    hidden = (jax.nn.silu(gate_pre) * lifted).astype(jnp.bfloat16)
    partial_value = jnp.einsum("necf,efd->necd", hidden, w_down, preferred_element_type=jnp.float32)
    summed = lax.psum_scatter(partial_value, "dp", scatter_dimension=3, tiled=True)
    expert_out = summed.astype(jnp.bfloat16)
    returned = lax.all_to_all(expert_out, "expert", split_axis=0, concat_axis=0, tiled=True)
    flattened = returned.reshape(experts * capacity, returned.shape[3])
    token_rows = jnp.dot(placing, flattened, preferred_element_type=jnp.float32)
    return (gating[:, None] * token_rows).astype(jnp.bfloat16)


def solution(mesh):
    in_specs = (
        P("expert", None),
        P("expert"),
        P(),
        P("expert", None, "dp"),
        P("expert", None, "dp"),
        P("expert", "dp", None),
    )
    out_specs = P("expert", "dp")
    return jax.shard_map(
        per_device, mesh=mesh, in_specs=in_specs, out_specs=out_specs, check_vma=False
    )
```

profile of v0, /device:TPU:1, one launch (start us, length us, event | category | flops | bytes accessed | tf_op | source)
XLA Modules:
  0.0 322.7 jit_solution(474853803545134916)
XLA Ops:
  6.5 0.0 copy-start
  6.5 0.0 reduce-scatter.4.cloned.1.call-start
  6.5 0.7 fusion.38
  7.3 0.1 copy.14
  7.4 0.2 reduce_window_sum.11
  7.6 0.1 copy.15
  7.6 0.7 select_reduce_fusion
  8.3 0.7 multiply_add_fusion
  9.0 2.9 convolution_convert_fusion
  11.9 2.4 reshape.33
  14.2 0.0 copy-start.6
  14.3 73.8 %all_to_all.10 = bf16[32,1,12,2048]{3,2,1,0:T(8,128)(2,1)S(1)} all-to-all(bf16[32,1,12,2048]{3,2,1,0:T(8,128)(2,1)S(1)} %bitcast.70), channel_id=1, replica_groups=mesh['dp'=32,'expert'=32] {'expert'}, dimensions={0} | all-to-all | bytes 3145728 | tf_op jit(solution)/shard_map/all_to_all | solution.py:30
  88.1 0.0 copy-start.1
  88.1 1.3 copy-done.1
  89.4 0.0 copy-done.6
  89.4 0.0 copy-start.3
  89.4 1.2 fusion.4
  90.6 0.0 copy-done
  90.6 0.0 copy-done.3
  90.7 5.1 %convolution_bitcast_fusion = f32[32,1,12,2048]{3,0,2,1:T(8,128)} fusion(bf16[1,256,2048]{2,1,0:T(8,128)(2,1)S(1)} %copy-done, bf16[32,1,12,2048]{3,2,1,0:T(8,128)(2,1)} %copy-done.1, bf16[1,2048,256]{2,1,0:T(8,128)(2,1)S(1)} %copy-done.3, f32[32,1,12,256]{3,0,2,1:T(8,128)S(1)} %fusion.4), kind=kOutput, calls=%fused_computation | convolution fusion | flops 805896192 | bytes 7208960 | tf_op jit(solution)/shard_map/necf,efd->necd/dot_general | solution.py:34
  95.8 12.2 %copy.19 = f32[32,1,12,2048]{0,2,1,3:T(8,128)} copy(f32[32,1,12,2048]{3,0,2,1:T(8,128)} %convolution_bitcast_fusion) | data formatting | bytes 6291456
  107.9 11.8 %reshape.43 = f32[2048,384]{1,0:T(8,128)} reshape(f32[2048,1,12,32]{3,2,1,0:T(8,128)} %bitcast.69) | data formatting | bytes 6291456
  119.7 0.0 copy-start.2
  119.7 0.0 copy-start.4
  119.7 0.0 copy-start.5
  119.7 0.0 reduce-scatter.4.cloned.1.call-update
  119.7 1.0 copy-done.2
  120.7 0.0 copy-done.4
  120.8 0.0 copy-done.5
  120.8 0.3 fusion.22
  121.1 143.9 %reduce-scatter.4.cloned.1.call-done = f32[64,384]{1,0:T(8,128)} async-done(((f32[2048,384]{1,0:T(8,128)}), f32[64,384]{1,0:T(8,128)}) %reduce-scatter.4.cloned.1.call-update) | async-done | bytes 98320
  265.0 1.1 reshape.44
  266.1 0.2 copy.20
  266.3 0.7 reshape.45
  267.1 35.9 %all-to-all-start.1 = ((bf16[32,2,384]{2,1,0:T(2,128)(2,1)}), bf16[32,2,384]{2,1,0:T(2,128)(2,1)S(1)}, u32[]{:S(2)}, u32[]{:S(2)}) async-start(bf16[32,2,384]{2,1,0:T(2,128)(2,1)} %reshape.45), calls=%async_computation.1 | async-start | bytes 98304 | tf_op jit(solution)/shard_map/all_to_all | solution.py:37
  303.0 11.8 %all-to-all-done.1 = bf16[32,2,384]{2,1,0:T(2,128)(2,1)S(1)} async-done(((bf16[32,2,384]{2,1,0:T(2,128)(2,1)}), bf16[32,2,384]{2,1,0:T(2,128)(2,1)S(1)}, u32[]{:S(2)}, u32[]{:S(2)}) %all-to-all-start.1) | async-done | bytes 49184 | tf_op jit(solution)/shard_map/all_to_all | solution.py:37
  314.8 0.1 reshape.46
  315.0 0.8 fusion.21
  (3 shorter events, 0.1 us)
Async XLA Ops:
  6.5 84.1 %copy-start = (bf16[1,256,2048]{2,1,0:T(8,128)(2,1)S(1)}, bf16[1,256,2048]{2,1,0:T(8,128)(2,1)}, u32[]{:S(2)}) copy-start(bf16[1,256,2048]{2,1,0:T(8,128)(2,1)} %param.11) | copy-start | bytes 3145732
  6.5 258.4 %reduce-scatter.4.cloned.1.call-start = ((), (), s32[]{:S(2)}) async-start(), calls=%async_computation.3 | async-start | bytes 3244032
  14.2 75.2 %copy-start.6 = (bf16[1,2048,256]{2,1,0:T(8,128)(2,1)S(1)}, bf16[1,2048,256]{2,1,0:T(8,128)(2,1)}, u32[]{:S(2)}) copy-start(bf16[1,2048,256]{2,1,0:T(8,128)(2,1)} %param.9) | copy-start | bytes 3145732
  88.1 1.3 copy-start.1
  89.4 1.2 copy-start.3
  119.7 1.0 copy-start.2
  119.7 1.1 copy-start.4
  119.7 1.1 copy-start.5
  267.1 47.7 %all-to-all-start.1 = ((bf16[32,2,384]{2,1,0:T(2,128)(2,1)}), bf16[32,2,384]{2,1,0:T(2,128)(2,1)S(1)}, u32[]{:S(2)}, u32[]{:S(2)}) async-start(bf16[32,2,384]{2,1,0:T(2,128)(2,1)} %reshape.45), calls=%async_computation.1 | async-start | bytes 98304 | tf_op jit(solution)/shard_map/all_to_all | solution.py:37
Sparse Core Ops, SparseCore 0:
  119.8 145.0 reduce-scatter.3
where the time goes:
time: 323 us
  waiting for transfers between devices  156 us (48%)
  blocking collectives  73.8 us (23%)
  starting transfers between devices  35.9 us (11%)
  local copies, waits for them, and re-layouts  31.1 us (10%)
  between operations  13.5 us (4%)
  matrix products  10.3 us (3%)
    unnamed x2, waiting for transfers between devices  144 us
    all_to_all x1, blocking collectives, per_device(): lax.all_to_all(outgoing, 'expert', split_axis=0, concat_axis=0, tiled=True)  73.8 us
    all_to_all x1, starting transfers between devices, per_device(): lax.all_to_all(expert_out, 'expert', split_axis=0, concat_axis=0, tiled=T...  35.9 us
    unnamed x20, local copies, waits for them, and re-layouts  28.5 us
    all_to_all x1, waiting for transfers between devices, per_device(): lax.all_to_all(expert_out, 'expert', split_axis=0, concat_axis=0, tiled=T...  11.8 us
  transfers between devices with their start and end apart: 2, of which 2 were waited for; matrix products, arithmetic and copies ran while one was open for 0% of the time, Pallas kernels for 0%

commit v1 on v0

v1 whole, which is shorter than its diff:
```python
import functools

import jax
import jax.numpy as jnp
from jax import lax
from jax.experimental import pallas as pl
from jax.experimental.pallas import tpu as pltpu
from jax.sharding import PartitionSpec as P

MESH = pl.DeviceIdType.MESH
CAP = 12
PAD = 16
RING = 8
BLOCKS = 3
PER = CAP // BLOCKS
F32 = jnp.float32
BF16 = jnp.bfloat16
NN = (((1,), (0,)), ((), ()))
NT = (((1,), (1,)), ((), ()))


def dot(a, b, dims=NN):
    return lax.dot_general(a, b, dims, preferred_element_type=F32)


def iota(shape, axis):
    return lax.broadcasted_iota(jnp.int32, shape, axis)


def kernel(
    ring, zs, es,
    ids_ref, tok_hbm, wr_hbm, wg_hbm, wu_hbm, wd_hbm, out_ref,
    tok, wr, wg, wu, wd, wdt, outg, inc, xb, gacc, uacc, hid,
    rs_out, rs_in, z_own, z_out, z_in, fin, r_out, r_in, placed_t, gate_col,
    load_sem, a_send, a_recv, ag_send, ag_recv, rs_send, rs_recv, z_send, z_recv, b_send, b_recv,
):
    me_dp = lax.axis_index("dp")
    me = lax.axis_index("expert")
    zl = me_dp // ring
    x = me_dp % ring
    half = ring // 2
    toks, width = tok.shape
    chunk = width // ring
    hidden = wg.shape[1]
    cols = width // (ring * zs)
    rows = es * PER
    slots = es * PAD

    loads = [
        pltpu.make_async_copy(src, dst, load_sem.at[i])
        for i, (src, dst) in enumerate(
            ((tok_hbm, tok), (wg_hbm, wg), (wu_hbm, wu), (wd_hbm, wd), (wr_hbm, wr))
        )
    ]
    for load in loads:
        load.start()

    right = zl * ring + (x + 1) % ring
    left = zl * ring + (x + ring - 1) % ring
    sides = (right, left)

    barrier = pltpu.get_barrier_semaphore()

    @pl.loop(1, es)
    def _(k):
        pl.semaphore_signal(barrier, inc=1, device_id={"expert": (me + k) % es}, device_id_type=MESH)

    for side in sides:
        pl.semaphore_signal(barrier, inc=1, device_id={"dp": side}, device_id_type=MESH)
    for k in range(1, zs):
        pl.semaphore_signal(
            barrier, inc=1, device_id={"dp": ((zl + k) % zs) * ring + x}, device_id_type=MESH
        )

    ids = ids_ref[...]
    onehot = (iota((es, toks), 0) == ids).astype(F32)
    before = (iota((toks, toks), 0) < iota((toks, toks), 1)).astype(BF16)
    rank = jnp.sum(dot(onehot.astype(BF16), before) * onehot, axis=0, keepdims=True)
    target = ((ids - me + es) % es) * PAD + rank.astype(jnp.int32)
    placing = (iota((slots, toks), 0) == target).astype(F32)

    loads[0].wait()
    mine = tok[:, pl.ds(pl.multiple_of(x * chunk, chunk), chunk)]
    sent = dot(placing.astype(BF16), mine).astype(BF16)
    outg[...] = sent.reshape(es, PAD, chunk)
    inc[0] = outg[0]

    pl.semaphore_wait(barrier, es - 1 + 2 + zs - 1)

    def dispatch(k):
        return pltpu.make_async_remote_copy(
            src_ref=outg.at[k], dst_ref=inc.at[k], send_sem=a_send, recv_sem=a_recv,
            device_id={"expert": (me + k) % es}, device_id_type=MESH,
        )

    @pl.loop(1, es)
    def _(k):
        dispatch(k).start()

    placed_t[...] = placing.T.astype(BF16)
    loads[4].wait()
    router = dot(tok[...], wr[...])
    picked = jnp.sum(router * onehot.T, axis=1, keepdims=True)
    gate_col[...] = jnp.broadcast_to(jax.nn.sigmoid(picked), gate_col.shape)
    loads[3].wait()
    for t in range(ring):
        for z in range(zs):
            start = (z * ring + t) * cols
            lo = start // 128 * 128
            tile = wd[:, lo:lo + 128].astype(F32).T
            wdt[t, z * cols:(z + 1) * cols, :] = tile[start - lo:start - lo + cols].astype(BF16)

    every = pl.ds(1, es - 1)
    pltpu.make_async_copy(inc.at[every], inc.at[every], a_recv).wait()

    def expand(b):
        i, r = iota((slots, rows), 0), iota((slots, rows), 1)
        return ((i // PAD == r // PER) & (i % PAD - b * PER == r % PER)).astype(BF16)

    def compact(b):
        r, i = iota((rows, slots), 0), iota((rows, slots), 1)
        return ((i // PAD == r // PER) & (i % PAD - b * PER == r % PER)).astype(BF16)

    def ag_hops(b):
        return (half, half - 1) if b % 2 == 0 else (half - 1, half)

    def rs_hops(b):
        return (half, half - 1) if b == 0 else (half - 1, half)

    def slot(way, step):
        return 0 if step == 0 else step + way * half

    def gather(way, step, b):
        return pltpu.make_async_remote_copy(
            src_ref=xb.at[slot(way, step - 1), b], dst_ref=xb.at[slot(way, step), b],
            send_sem=ag_send.at[way, step - 1, b], recv_sem=ag_recv.at[way, step - 1, b],
            device_id={"dp": sides[way]}, device_id_type=MESH,
        )

    def add_chunk(b, at, origin):
        block = xb[at, b]
        depth = pl.ds(pl.multiple_of(origin * chunk, chunk), chunk)
        g = dot(block, wg[depth, :])
        u = dot(block, wu[depth, :])
        if at == 0:
            gacc[b] = g
            uacc[b] = u
        else:
            gacc[b] += g
            uacc[b] += u

    packed = inc[...].reshape(slots, chunk)
    for b in range(BLOCKS):
        xb[0, b] = dot(compact(b), packed).astype(BF16)
        for way in range(2):
            gather(way, 1, b).start()
    loads[1].wait()
    loads[2].wait()
    for b in range(BLOCKS):
        add_chunk(b, 0, x)
    for step in range(1, half + 1):
        for b in range(BLOCKS):
            for way in range(2):
                hops = ag_hops(b)[way]
                if step > hops:
                    continue
                gather(way, step, b).wait_recv()
                if step < hops:
                    gather(way, step + 1, b).start()
                origin = (x + ring - step) % ring if way == 0 else (x + step) % ring
                add_chunk(b, slot(way, step), origin)

    def scatter(way, step, b):
        return pltpu.make_async_remote_copy(
            src_ref=rs_out.at[way, step - 1, b], dst_ref=rs_in.at[way, step - 1, b],
            send_sem=rs_send.at[way, step - 1, b], recv_sem=rs_recv.at[way, step - 1, b],
            device_id={"dp": sides[way]}, device_id_type=MESH,
        )

    def partial(b, t):
        return dot(wdt[t], hid[b], NT)

    def toward(way, distance):
        return (x + distance) % ring if way == 0 else (x + ring - distance) % ring

    for b in range(BLOCKS):
        g = gacc[b]
        hid[b] = (g / (1.0 + jnp.exp(-g)) * uacc[b]).astype(BF16)
        for way in range(2):
            rs_out[way, 0, b] = partial(b, toward(way, rs_hops(b)[way])).astype(BF16)
            scatter(way, 1, b).start()
    for step in range(2, half + 1):
        for b in range(BLOCKS):
            for way in range(2):
                hops = rs_hops(b)[way]
                if step > hops:
                    continue
                own = partial(b, toward(way, hops - step + 1))
                scatter(way, step - 1, b).wait_recv()
                rs_out[way, step - 1, b] = (own + rs_in[way, step - 2, b].astype(F32)).astype(BF16)
                scatter(way, step, b).start()

    def across(k, b):
        return pltpu.make_async_remote_copy(
            src_ref=z_out.at[b, (zl + k) % zs], dst_ref=z_in.at[b, k - 1],
            send_sem=z_send.at[k - 1, b], recv_sem=z_recv.at[k - 1, b],
            device_id={"dp": ((zl + k) % zs) * ring + x}, device_id_type=MESH,
        )

    for b in range(BLOCKS):
        total = partial(b, x)
        for way in range(2):
            hops = rs_hops(b)[way]
            scatter(way, hops, b).wait_recv()
            total = total + rs_in[way, hops - 1, b].astype(F32)
        total = total.reshape(zs, cols, rows)
        z_own[b] = total
        z_out[b] = total.astype(BF16)
        for k in range(1, zs):
            across(k, b).start()

    back = jnp.zeros((slots, 128), F32)
    for b in range(BLOCKS):
        total = z_own[b, zl]
        for k in range(1, zs):
            across(k, b).wait_recv()
            total = total + z_in[b, k - 1].astype(F32)
        fin[0:cols] = total.astype(BF16)
        if cols < 128:
            fin[cols:128] = jnp.zeros((128 - cols, rows), BF16)
        back = back + dot(expand(b), fin[...], NT)
    r_out[...] = back.astype(BF16).reshape(es, PAD, 128)
    r_in[0] = r_out[0]

    def give_back(k):
        return pltpu.make_async_remote_copy(
            src_ref=r_out.at[k], dst_ref=r_in.at[k], send_sem=b_send, recv_sem=b_recv,
            device_id={"expert": (me + es - k) % es}, device_id_type=MESH,
        )

    @pl.loop(1, es)
    def _(k):
        give_back(k).start()

    pltpu.make_async_copy(outg.at[every], outg.at[every], a_send).wait()
    for b in range(BLOCKS):
        for way in range(2):
            for step in range(1, ag_hops(b)[way] + 1):
                gather(way, step, b).wait_send()
            for step in range(1, rs_hops(b)[way] + 1):
                scatter(way, step, b).wait_send()
        for k in range(1, zs):
            across(k, b).wait_send()

    pltpu.make_async_copy(r_in.at[every], r_in.at[every], b_recv).wait()
    found = dot(placed_t[...], r_in[...].reshape(slots, 128))
    out_ref[...] = (gate_col[...] * found)[:, :cols].astype(BF16)
    pltpu.make_async_copy(r_out.at[every], r_out.at[every], b_send).wait()


def per_device(ring, zs, es, tokens, expert_ids, w_router, w_gate, w_up, w_down):
    toks, width = tokens.shape
    hidden = w_gate.shape[2]
    chunk = width // ring
    cols = width // (ring * zs)
    rows = es * PER
    half = ring // 2
    any_space = pl.BlockSpec(memory_space=pl.ANY)
    vmem = pl.BlockSpec(memory_space=pltpu.VMEM)
    dma = pltpu.SemaphoreType.DMA
    return pl.pallas_call(
        functools.partial(kernel, ring, zs, es),
        out_shape=jax.ShapeDtypeStruct((toks, cols), BF16),
        in_specs=[vmem] + [any_space] * 5,
        out_specs=vmem,
        scratch_shapes=[
            pltpu.VMEM((toks, width), BF16),
            pltpu.VMEM(w_router.shape, BF16),
            pltpu.VMEM((width, hidden), BF16),
            pltpu.VMEM((width, hidden), BF16),
            pltpu.VMEM((hidden, width), BF16),
            pltpu.VMEM((ring, zs * cols, hidden), BF16),
            pltpu.VMEM((es, PAD, chunk), BF16),
            pltpu.VMEM((es, PAD, chunk), BF16),
            pltpu.VMEM((ring + 1, BLOCKS, rows, chunk), BF16),
            pltpu.VMEM((BLOCKS, rows, hidden), F32),
            pltpu.VMEM((BLOCKS, rows, hidden), F32),
            pltpu.VMEM((BLOCKS, rows, hidden), BF16),
            pltpu.VMEM((2, half, BLOCKS, zs * cols, rows), BF16),
            pltpu.VMEM((2, half, BLOCKS, zs * cols, rows), BF16),
            pltpu.VMEM((BLOCKS, zs, cols, rows), F32),
            pltpu.VMEM((BLOCKS, zs, cols, rows), BF16),
            pltpu.VMEM((BLOCKS, max(zs - 1, 1), cols, rows), BF16),
            pltpu.VMEM((128, rows), BF16),
            pltpu.VMEM((es, PAD, 128), BF16),
            pltpu.VMEM((es, PAD, 128), BF16),
            pltpu.VMEM((toks, es * PAD), BF16),
            pltpu.VMEM((toks, 128), F32),
            dma((5,)),
            dma, dma,
            dma((2, half, BLOCKS)), dma((2, half, BLOCKS)),
            dma((2, half, BLOCKS)), dma((2, half, BLOCKS)),
            dma((max(zs - 1, 1), BLOCKS)), dma((max(zs - 1, 1), BLOCKS)),
            dma, dma,
        ],
        compiler_params=pltpu.CompilerParams(
            collective_id=0, has_side_effects=True, vmem_limit_bytes=56 * 2**20
        ),
        cost_estimate=pl.CostEstimate(
            flops=6 * BLOCKS * rows * width * hidden, bytes_accessed=6 * width * hidden, transcendentals=0
        ),
    )(
        expert_ids.reshape(1, toks), tokens, w_router, w_gate.reshape(width, hidden),
        w_up.reshape(width, hidden), w_down.reshape(hidden, width),
    )


def solution(mesh):
    es = mesh.shape["expert"]
    zs = mesh.shape["dp"] // RING
    in_specs = (
        P("expert", None),
        P("expert"),
        P(),
        P("expert", None, "dp"),
        P("expert", None, "dp"),
        P("expert", "dp", None),
    )
    return jax.shard_map(
        functools.partial(per_device, RING, zs, es), mesh=mesh, in_specs=in_specs,
        out_specs=P("expert", "dp"), check_vma=False,
    )
```

time: 323 us -> 92.5 us (0.29)
  waiting for transfers between devices: 156 us -> 0 us
  Pallas kernels: 0 us -> 89 us
  blocking collectives: 73.8 us -> 0 us
  starting transfers between devices: 35.9 us -> 0 us
  local copies, waits for them, and re-layouts: 31.1 us -> 3.35 us
  between operations: 13.5 us -> 0.01 us
  matrix products: 10.3 us -> 0 us
    unnamed x2 -> x0, waiting for transfers between devices: 144 us -> none
    pallas_call x0 -> x1, Pallas kernels: none -> 89 us  [per_device(): pl.pallas_call(functools.partial(kernel, ring, zs, es), out_shape=jax.Sha...]
    all_to_all x1 -> x0, blocking collectives: 73.8 us -> none  [per_device(): lax.all_to_all(outgoing, 'expert', split_axis=0, concat_axis=0, tiled=True)]
    all_to_all x1 -> x0, starting transfers between devices: 35.9 us -> none  [per_device(): lax.all_to_all(expert_out, 'expert', split_axis=0, concat_axis=0, tiled=T...]
    unnamed x20 -> x1, local copies, waits for them, and re-layouts: 28.5 us -> 1.9 us
    all_to_all x1 -> x0, waiting for transfers between devices: 11.8 us -> none  [per_device(): lax.all_to_all(expert_out, 'expert', split_axis=0, concat_axis=0, tiled=T...]
    dot_general x5 -> x0, matrix products: 10.3 us -> none  [the longest x1 5.09 us: per_device(): jnp.einsum('necf,efd->necd', hidden, w_down, preferred_element_type=jnp.f...]
  transfers between devices with their start and end apart: 2 -> 0, of which waited for: 2 -> 0; matrix products, arithmetic and copies ran while one was open for 0% -> 0% of each run, Pallas kernels for 0% -> 0%
where the time goes in v1:
time: 92.5 us; the launch traced here: 92.3 us
  Pallas kernels  89 us (96%)
  local copies, waits for them, and re-layouts  3.35 us (4%)
    pallas_call x1, Pallas kernels, per_device(): pl.pallas_call(functools.partial(kernel, ring, zs, es), out_shape=jax.Sha...  89 us
    unnamed x1, local copies, waits for them, and re-layouts  1.9 us

profile of v1, /device:TPU:1, one launch (start us, length us, event | category | flops | bytes accessed | tf_op | source)
XLA Modules:
  0.0 92.3 jit_solution(4572928418877601661)
XLA Ops:
  0.0 1.9 %copy.7.wr_hbm = bf16[2048,32]{1,0:T(8,128)(2,1)} copy(bf16[2048,32]{0,1:T(8,128)(2,1)} %param.8) | data formatting | bytes 262144 | tf_op args[2]
  1.9 89.0 %shard_map.64 = bf16[128,64]{1,0:T(8,128)(2,1)} custom-call(s32[1,128]{1,0:T(1,128)} %bitcast.7, bf16[128,2048]{1,0:T(8,128)(2,1)} %tok_hbm.1, bf16[2048,32]{1,0:T(8,128)(2,1)} %copy.7.wr_hbm, bf16[2048,256]{1,0:T(8,128)(2,1)} %bitcast.4, bf16[2048,256]{1,0:T(8,128)(2,1)} %bitcast.5, bf16[256,2048]{1,0:T(8,128)(2,1)} %bitcast.6), custom_call_target="tpu_custom_call" | custom-call | flops 1207959552 | bytes 3145728 | tf_op jit(solution)/shard_map/pallas_call | solution.py:271
  90.9 1.4 %copy.8 = bf16[128,64]{0,1:T(8,128)(2,1)} copy(bf16[128,64]{1,0:T(8,128)(2,1)} %shard_map.64) | data formatting | bytes 32768 | tf_op jit(solution)/shard_map/pallas_call | solution.py:271

commit v2 on v1

v2 whole, which is shorter than its diff:
```python
import functools

import jax
import jax.numpy as jnp
from jax import lax
from jax.experimental import pallas as pl
from jax.experimental.pallas import tpu as pltpu
from jax.sharding import PartitionSpec as P

MESH = pl.DeviceIdType.MESH
CAP = 12
PAD = 16
RING = 8
GROUP = 8
LANES = 128
F32 = jnp.float32
BF16 = jnp.bfloat16
NN = (((1,), (0,)), ((), ()))
NT = (((1,), (1,)), ((), ()))


def dot(a, b, dims=NN):
    return lax.dot_general(a, b, dims, preferred_element_type=F32)


def iota(shape, axis):
    return lax.broadcasted_iota(jnp.int32, shape, axis)


def kernel(
    ring, zs, es,
    ids_hbm, tok_hbm, wr_hbm, wg_hbm, wu_hbm, wd_hbm, out_ref,
    ids_ref, own_tok, tok, wr, wg, wu, wd, wdt, outg, inc, xb, gacc, uacc, hid,
    rs_out, rs_in, z_own, z_out, z_in, fin, r_out, r_in, gate_row, placed, pick,
    load_sem, a_send, a_recv, ag_send, ag_recv, rs_send, rs_recv, z_send, z_recv, b_send, b_recv,
):
    me_dp = lax.axis_index("dp")
    me = lax.axis_index("expert")
    zl = me_dp // ring
    x = me_dp % ring
    half = ring // 2
    toks, width = tok.shape
    chunk = width // ring
    cols = width // (ring * zs)
    slots = es * PAD
    groups = es // GROUP
    grows = GROUP * CAP
    gslots = GROUP * PAD
    blocks = es * CAP // LANES
    far = ring - 1
    mine = pl.ds(pl.multiple_of(x * chunk, chunk), chunk)
    across_x = (x + half) % ring
    theirs = pl.ds(pl.multiple_of(across_x * chunk, chunk), chunk)

    loads = [
        pltpu.make_async_copy(src, dst, load_sem.at[i])
        for i, (src, dst) in enumerate((
            (tok_hbm.at[:, mine], own_tok), (tok_hbm, tok), (wr_hbm, wr),
            (wd_hbm, wd), (wg_hbm, wg), (wu_hbm, wu), (ids_hbm, ids_ref),
        ))
    ]
    for i in (6, 0, 1, 3, 4, 5, 2):
        loads[i].start()

    sides = (zl * ring + (x + 1) % ring, zl * ring + (x + ring - 1) % ring)
    barrier = pltpu.get_barrier_semaphore()

    @pl.loop(1, es)
    def _(k):
        pl.semaphore_signal(barrier, inc=1, device_id={"expert": me ^ k}, device_id_type=MESH)

    for side in sides:
        pl.semaphore_signal(barrier, inc=1, device_id={"dp": side}, device_id_type=MESH)
    for k in range(1, zs):
        pl.semaphore_signal(
            barrier, inc=1, device_id={"dp": ((zl + k) % zs) * ring + x}, device_id_type=MESH
        )

    loads[6].wait()
    ids = ids_ref[...]
    onehot = (iota((es, toks), 0) == ids).astype(F32)
    before = (iota((toks, toks), 0) < iota((toks, toks), 1)).astype(BF16)
    rank = jnp.sum(dot(onehot.astype(BF16), before) * onehot, axis=0, keepdims=True)
    target = (ids ^ me) * PAD + rank.astype(jnp.int32)
    placing = (iota((slots, toks), 0) == target).astype(F32)
    placed[...] = placing.astype(BF16)

    loads[0].wait()
    outg[0] = dot(placed[...], own_tok[...]).astype(BF16).reshape(es, PAD, chunk)

    pl.semaphore_wait(barrier, es - 1 + 2 + zs - 1)

    def dispatch(which, g, k):
        return pltpu.make_async_remote_copy(
            src_ref=outg.at[which, k], dst_ref=inc.at[which, k],
            send_sem=a_send.at[which, g], recv_sem=a_recv.at[which, g],
            device_id={"expert": me ^ k}, device_id_type=MESH,
        )

    def send_group(which, g):
        @pl.loop(max(g * GROUP, 1), (g + 1) * GROUP)
        def _(k):
            dispatch(which, g, k).start()

    def group_bytes(ref, which, g, sem):
        part = ref.at[which, pl.ds(max(g * GROUP, 1), GROUP - (g == 0))]
        return pltpu.make_async_copy(part, part, sem.at[which, g])

    for g in range(groups):
        send_group(0, g)

    inc[0, 0] = outg[0, 0]
    loads[1].wait()
    outg[1] = dot(placed[...], tok[:, theirs]).astype(BF16).reshape(es, PAD, chunk)
    inc[1, 0] = outg[1, 0]

    def spread(shape, source_axis):
        i, r = iota(shape, source_axis), iota(shape, 1 - source_axis)
        rank_at = i & (PAD - 1)
        return ((lax.shift_right_logical(i, 4) * CAP + rank_at == r) & (rank_at < CAP)).astype(BF16)

    compact = spread((grows, gslots), 1)
    pick[...] = spread(pick.shape, 0)

    def slot(way, step):
        return 0 if step == 0 else step + way * (half - 1)

    def gather(way, step, g):
        return pltpu.make_async_remote_copy(
            src_ref=xb.at[slot(way, step - 1), g], dst_ref=xb.at[slot(way, step), g],
            send_sem=ag_send.at[way, step - 1, g], recv_sem=ag_recv.at[way, step - 1, g],
            device_id={"dp": sides[way]}, device_id_type=MESH,
        )

    def arrived(which, at, g):
        group_bytes(inc, which, g, a_recv).wait()
        part = inc[which, g * GROUP:(g + 1) * GROUP].reshape(gslots, chunk)
        xb[at, g] = dot(compact, part).astype(BF16)

    def add_chunk(g, at, origin):
        block = xb[at, g]
        depth = pl.ds(pl.multiple_of(origin * chunk, chunk), chunk)
        gate = dot(block, wg[depth, :])
        up = dot(block, wu[depth, :])
        span = slice(g * grows, (g + 1) * grows)
        if at == 0:
            gacc[span] = gate
            uacc[span] = up
        else:
            gacc[span] += gate
            uacc[span] += up

    def rs_hops(b):
        return (half, half - 1) if b % 2 == 0 else (half - 1, half)

    def scatter(way, step, b):
        return pltpu.make_async_remote_copy(
            src_ref=rs_out.at[way, step - 1, b], dst_ref=rs_in.at[way, step - 1, b],
            send_sem=rs_send.at[way, step - 1, b], recv_sem=rs_recv.at[way, step - 1, b],
            device_id={"dp": sides[way]}, device_id_type=MESH,
        )

    def partial(b, t):
        return dot(wdt[t], hid[b], NT)

    def toward(way, distance):
        return (x + distance) % ring if way == 0 else (x + ring - distance) % ring

    def arrive(g):
        arrived(0, 0, g)
        for way in range(2):
            gather(way, 1, g).start()

    def hop(step, g):
        for way in range(2):
            gather(way, step, g).wait_recv()
            if step < half - 1:
                gather(way, step + 1, g).start()
            origin = (x + ring - step) % ring if way == 0 else (x + step) % ring
            add_chunk(g, slot(way, step), origin)

    def opposite(g):
        arrived(1, far, g)
        add_chunk(g, far, across_x)

    def begin_sums(b):
        gate = gacc[b * LANES:(b + 1) * LANES]
        up = uacc[b * LANES:(b + 1) * LANES]
        hid[b] = (gate / (1.0 + jnp.exp(-gate)) * up).astype(BF16)
        for way in range(2):
            rs_out[way, 0, b] = partial(b, toward(way, rs_hops(b)[way])).astype(BF16)
            scatter(way, 1, b).start()

    def send_opposite():
        for g in range(groups):
            send_group(1, g)

    def prepare():
        loads[3].wait()
        for t in range(ring):
            for z in range(zs):
                start = (z * ring + t) * cols
                lo = start // 128 * 128
                tile = wd[:, lo:lo + 128].astype(F32).T
                wdt[t, z * cols:(z + 1) * cols, :] = tile[start - lo:start - lo + cols].astype(BF16)

    def own_chunk(g):
        if g == 0:
            loads[4].wait()
            loads[5].wait()
        add_chunk(g, 0, x)

    steps = [(half - 2.8, 0, send_opposite, ()), (half - 2.4, 0, prepare, ())]
    for g in range(groups):
        late = 0 if 2 * g < groups else 1.5
        steps.append((late, g, arrive, (g,)))
        steps.append((late + 0.1, g, own_chunk, (g,)))
        for step in range(1, half):
            steps.append((late + step, g, hop, (step, g)))
        steps.append((late + half - 1.4, g, opposite, (g,)))
    for b in range(blocks):
        last = ((b + 1) * LANES - 1) // grows
        late = 0 if 2 * last < groups else 1.5
        steps.append((late + half - 0.9, b, begin_sums, (b,)))
    for _, _, action, given in sorted(steps, key=lambda entry: entry[:2]):
        action(*given)

    loads[2].wait()
    router = dot(wr[...], tok[...], NT)
    picked = jnp.sum(router * (iota((es, toks), 0) == ids_ref[...]).astype(F32), axis=0, keepdims=True)
    gate_row[...] = jnp.broadcast_to(jax.nn.sigmoid(picked), gate_row.shape)

    for step in range(2, half + 1):
        for b in range(blocks):
            for way in range(2):
                hops = rs_hops(b)[way]
                if step > hops:
                    continue
                own = partial(b, toward(way, hops - step + 1))
                scatter(way, step - 1, b).wait_recv()
                rs_out[way, step - 1, b] = (own + rs_in[way, step - 2, b].astype(F32)).astype(BF16)
                scatter(way, step, b).start()

    def across(k, b):
        return pltpu.make_async_remote_copy(
            src_ref=z_out.at[b, (zl + k) % zs], dst_ref=z_in.at[b, k - 1],
            send_sem=z_send.at[k - 1, b], recv_sem=z_recv.at[k - 1, b],
            device_id={"dp": ((zl + k) % zs) * ring + x}, device_id_type=MESH,
        )

    for b in range(blocks):
        total = partial(b, x)
        for way in range(2):
            hops = rs_hops(b)[way]
            scatter(way, hops, b).wait_recv()
            total = total + rs_in[way, hops - 1, b].astype(F32)
        total = total.reshape(zs, cols, LANES)
        z_out[b] = total.astype(BF16)
        for k in range(1, zs):
            across(k, b).start()
        z_own[b] = total

    def give_back(k):
        return pltpu.make_async_remote_copy(
            src_ref=r_out.at[k], dst_ref=r_in.at[k], send_sem=b_send, recv_sem=b_recv,
            device_id={"expert": me ^ k}, device_id_type=MESH,
        )

    fin[...] = jnp.zeros_like(fin)
    first = 0
    for b in range(blocks):
        total = z_own[b, zl]
        for k in range(1, zs):
            across(k, b).wait_recv()
            total = total + z_in[b, k - 1].astype(F32)
        fin[b, 0:cols] = total.astype(BF16)
        last = (b + 1) * LANES // CAP
        back = jnp.zeros(((last - first) * PAD, 128), F32)
        for c in range(first * CAP // LANES, b + 1):
            part = pick[first * PAD:last * PAD, c * LANES:(c + 1) * LANES]
            back = back + dot(part, fin[c], NT)
        r_out[first:last] = back.astype(BF16).reshape(last - first, PAD, 128)

        @pl.loop(max(first, 1), last)
        def _(k):
            give_back(k).start()

        first = last

    r_in[0] = r_out[0]
    for which in range(2):
        for g in range(groups):
            group_bytes(outg, which, g, a_send).wait()
    for way in range(2):
        for step in range(1, half):
            for g in range(groups):
                gather(way, step, g).wait_send()
        for b in range(blocks):
            for step in range(1, rs_hops(b)[way] + 1):
                scatter(way, step, b).wait_send()
    for b in range(blocks):
        for k in range(1, zs):
            across(k, b).wait_send()

    every = pl.ds(1, es - 1)
    pltpu.make_async_copy(r_in.at[every], r_in.at[every], b_recv).wait()
    back = r_in[...].reshape(slots, 128)
    found = lax.dot_general(placed[...], back, (((0,), (0,)), ((), ())), preferred_element_type=F32)
    out_ref[...] = (gate_row[0:1] * found.T[:cols]).astype(BF16)
    pltpu.make_async_copy(r_out.at[every], r_out.at[every], b_send).wait()


def per_device(ring, zs, es, tokens, expert_ids, w_router, w_gate, w_up, w_down):
    toks, width = tokens.shape
    hidden = w_gate.shape[2]
    chunk = width // ring
    cols = width // (ring * zs)
    half = ring // 2
    rows = es * CAP
    groups = es // GROUP
    blocks = rows // LANES
    zn = max(zs - 1, 1)
    any_space = pl.BlockSpec(memory_space=pl.ANY)
    vmem = pl.BlockSpec(memory_space=pltpu.VMEM)
    dma = pltpu.SemaphoreType.DMA
    out = pl.pallas_call(
        functools.partial(kernel, ring, zs, es),
        out_shape=jax.ShapeDtypeStruct((cols, toks), BF16),
        in_specs=[any_space] * 6,
        out_specs=vmem,
        scratch_shapes=[
            pltpu.VMEM((1, toks), jnp.int32),
            pltpu.VMEM((toks, chunk), BF16),
            pltpu.VMEM((toks, width), BF16),
            pltpu.VMEM((es, width), BF16),
            pltpu.VMEM((width, hidden), BF16),
            pltpu.VMEM((width, hidden), BF16),
            pltpu.VMEM((hidden, width), BF16),
            pltpu.VMEM((ring, zs * cols, hidden), BF16),
            pltpu.VMEM((2, es, PAD, chunk), BF16),
            pltpu.VMEM((2, es, PAD, chunk), BF16),
            pltpu.VMEM((ring, groups, GROUP * CAP, chunk), BF16),
            pltpu.VMEM((rows, hidden), F32),
            pltpu.VMEM((rows, hidden), F32),
            pltpu.VMEM((blocks, LANES, hidden), BF16),
            pltpu.VMEM((2, half, blocks, zs * cols, LANES), BF16),
            pltpu.VMEM((2, half, blocks, zs * cols, LANES), BF16),
            pltpu.VMEM((blocks, zs, cols, LANES), F32),
            pltpu.VMEM((blocks, zs, cols, LANES), BF16),
            pltpu.VMEM((blocks, zn, cols, LANES), BF16),
            pltpu.VMEM((blocks, 128, LANES), BF16),
            pltpu.VMEM((es, PAD, 128), BF16),
            pltpu.VMEM((es, PAD, 128), BF16),
            pltpu.VMEM((8, toks), F32),
            pltpu.VMEM((es * PAD, toks), BF16),
            pltpu.VMEM((es * PAD, rows), BF16),
            dma((7,)),
            dma((2, groups)), dma((2, groups)),
            dma((2, half - 1, groups)), dma((2, half - 1, groups)),
            dma((2, half, blocks)), dma((2, half, blocks)),
            dma((zn, blocks)), dma((zn, blocks)),
            dma, dma,
        ],
        compiler_params=pltpu.CompilerParams(
            collective_id=0, has_side_effects=True, vmem_limit_bytes=56 * 2**20
        ),
        cost_estimate=pl.CostEstimate(
            flops=6 * rows * width * hidden, bytes_accessed=6 * width * hidden, transcendentals=0
        ),
    )(
        expert_ids.reshape(1, toks), tokens, w_router.T, w_gate.reshape(width, hidden),
        w_up.reshape(width, hidden), w_down.reshape(hidden, width),
    )
    return out.T


def solution(mesh):
    es = mesh.shape["expert"]
    zs = mesh.shape["dp"] // RING
    in_specs = (
        P("expert", None),
        P("expert"),
        P(),
        P("expert", None, "dp"),
        P("expert", None, "dp"),
        P("expert", "dp", None),
    )
    return jax.shard_map(
        functools.partial(per_device, RING, zs, es), mesh=mesh, in_specs=in_specs,
        out_specs=P("expert", "dp"), check_vma=False,
    )
```

time: 92.5 us -> 82.5 us (0.89)
  Pallas kernels: 89 us -> 81 us
  local copies, waits for them, and re-layouts: 3.35 us -> 1.32 us
    pallas_call x1, Pallas kernels: 89 us -> 81 us  [per_device(): pl.pallas_call(functools.partial(kernel, ring, zs, es), out_shape=jax.Sha...]
    pallas_call x1 -> x0, local copies, waits for them, and re-layouts: 1.45 us -> none  [per_device(): pl.pallas_call(functools.partial(kernel, ring, zs, es), out_shape=jax.Sha...]
where the time goes in v2:
time: 82.5 us; the launch traced here: 82.3 us
  Pallas kernels  81 us (98%)
  local copies, waits for them, and re-layouts  1.32 us (2%)
    pallas_call x1, Pallas kernels, per_device(): pl.pallas_call(functools.partial(kernel, ring, zs, es), out_shape=jax.Sha...  81 us

profile of v2, /device:TPU:1, one launch (start us, length us, event | category | flops | bytes accessed | tf_op | source)
XLA Modules:
  0.0 82.3 jit_solution(15169592047845201210)
XLA Ops:
  0.0 81.0 %shard_map.64 = bf16[64,128]{1,0:T(8,128)(2,1)} custom-call(s32[1,128]{1,0:T(1,128)} %bitcast.11, bf16[128,2048]{1,0:T(8,128)(2,1)} %tok_hbm.1, bf16[32,2048]{1,0:T(8,128)(2,1)} %bitcast.10, bf16[2048,256]{1,0:T(8,128)(2,1)} %bitcast.7, bf16[2048,256]{1,0:T(8,128)(2,1)} %bitcast.8, bf16[256,2048]{1,0:T(8,128)(2,1)} %bitcast.9), custom_call_target="tpu_custom_call" | custom-call | flops 1207959552 | bytes 3145728 | tf_op jit(solution)/shard_map/pallas_call | solution.py:326
  81.0 1.3 %copy.8 = bf16[128,64]{0,1:T(8,128)(2,1)} copy(bf16[128,64]{0,1:T(8,128)(2,1)} %bitcast.6) | data formatting | bytes 32768

commit v3 on v2

--- a/solution.py
+++ b/solution.py
@@ -12,7 +12,7 @@
 PAD = 16
 RING = 8
 GROUP = 8
-LANES = 128
+LANES = 384
 F32 = jnp.float32
 BF16 = jnp.bfloat16
 NN = (((1,), (0,)), ((), ()))
@@ -31,7 +31,7 @@
     ring, zs, es,
     ids_hbm, tok_hbm, wr_hbm, wg_hbm, wu_hbm, wd_hbm, out_ref,
     ids_ref, own_tok, tok, wr, wg, wu, wd, wdt, outg, inc, xb, gacc, uacc, hid,
-    rs_out, rs_in, z_own, z_out, z_in, fin, r_out, r_in, gate_row, placed, pick,
+    rs_out, rs_in, z_own, z_out, z_in, fin, r_out, r_in, gate_row, placed, placed_t, pick,
     load_sem, a_send, a_recv, ag_send, ag_recv, rs_send, rs_recv, z_send, z_recv, b_send, b_recv,
 ):
     me_dp = lax.axis_index("dp")
@@ -110,9 +110,13 @@
         send_group(0, g)
 
     inc[0, 0] = outg[0, 0]
-    loads[1].wait()
-    outg[1] = dot(placed[...], tok[:, theirs]).astype(BF16).reshape(es, PAD, chunk)
-    inc[1, 0] = outg[1, 0]
+    loads[3].wait()
+    for t in range(ring):
+        for z in range(zs):
+            start = (z * ring + t) * cols
+            lo = start // 128 * 128
+            tile = wd[:, lo:lo + 128].astype(F32).T
+            wdt[t, z * cols:(z + 1) * cols, :] = tile[start - lo:start - lo + cols].astype(BF16)
 
     def spread(shape, source_axis):
         i, r = iota(shape, source_axis), iota(shape, 1 - source_axis)
@@ -120,7 +124,6 @@
         return ((lax.shift_right_logical(i, 4) * CAP + rank_at == r) & (rank_at < CAP)).astype(BF16)
 
     compact = spread((grows, gslots), 1)
-    pick[...] = spread(pick.shape, 0)
 
     def slot(way, step):
         return 0 if step == 0 else step + way * (half - 1)
@@ -192,17 +195,11 @@
             scatter(way, 1, b).start()
 
     def send_opposite():
+        loads[1].wait()
+        outg[1] = dot(placed[...], tok[:, theirs]).astype(BF16).reshape(es, PAD, chunk)
+        inc[1, 0] = outg[1, 0]
         for g in range(groups):
             send_group(1, g)
-
-    def prepare():
-        loads[3].wait()
-        for t in range(ring):
-            for z in range(zs):
-                start = (z * ring + t) * cols
-                lo = start // 128 * 128
-                tile = wd[:, lo:lo + 128].astype(F32).T
-                wdt[t, z * cols:(z + 1) * cols, :] = tile[start - lo:start - lo + cols].astype(BF16)
 
     def own_chunk(g):
         if g == 0:
@@ -210,7 +207,70 @@
             loads[5].wait()
         add_chunk(g, 0, x)
 
-    steps = [(half - 2.8, 0, send_opposite, ()), (half - 2.4, 0, prepare, ())]
+    def gates():
+        loads[2].wait()
+        router = dot(wr[...], tok[...], NT)
+        chosen = (iota((es, toks), 0) == ids_ref[...]).astype(F32)
+        picked = jnp.sum(router * chosen, axis=0, keepdims=True)
+        gate_row[...] = jnp.broadcast_to(jax.nn.sigmoid(picked), gate_row.shape)
+        placed_t[...] = placed[...].astype(F32).T.astype(BF16)
+        pick[...] = spread(pick.shape, 0)
+        fin[...] = jnp.zeros_like(fin)
+
+    def sums(step, b):
+        for way in range(2):
+            hops = rs_hops(b)[way]
+            if step > hops:
+                continue
+            own = partial(b, toward(way, hops - step + 1))
+            scatter(way, step - 1, b).wait_recv()
+            rs_out[way, step - 1, b] = (own + rs_in[way, step - 2, b].astype(F32)).astype(BF16)
+            scatter(way, step, b).start()
+
+    def across(k, b):
+        return pltpu.make_async_remote_copy(
+            src_ref=z_out.at[b, (zl + k) % zs], dst_ref=z_in.at[b, k - 1],
+            send_sem=z_send.at[k - 1, b], recv_sem=z_recv.at[k - 1, b],
+            device_id={"dp": ((zl + k) % zs) * ring + x}, device_id_type=MESH,
+        )
+
+    def finish(b):
+        total = partial(b, x)
+        for way in range(2):
+            hops = rs_hops(b)[way]
+            scatter(way, hops, b).wait_recv()
+            total = total + rs_in[way, hops - 1, b].astype(F32)
+        total = total.reshape(zs, cols, LANES)
+        z_out[b] = total.astype(BF16)
+        for k in range(1, zs):
+            across(k, b).start()
+        z_own[b] = total
+
+    def give_back(k):
+        return pltpu.make_async_remote_copy(
+            src_ref=r_out.at[k], dst_ref=r_in.at[k], send_sem=b_send, recv_sem=b_recv,
+            device_id={"expert": me ^ k}, device_id_type=MESH,
+        )
+
+    def close(b):
+        total = z_own[b, zl]
+        for k in range(1, zs):
+            across(k, b).wait_recv()
+            total = total + z_in[b, k - 1].astype(F32)
+        fin[b, 0:cols] = total.astype(BF16)
+        first = b * LANES // CAP
+        last = (b + 1) * LANES // CAP
+        back = jnp.zeros(((last - first) * PAD, 128), F32)
+        for c in range(first * CAP // LANES, b + 1):
+            part = pick[first * PAD:last * PAD, c * LANES:(c + 1) * LANES]
+            back = back + dot(part, fin[c], NT)
+        r_out[first:last] = back.astype(BF16).reshape(last - first, PAD, 128)
+
+        @pl.loop(max(first, 1), last)
+        def _(k):
+            give_back(k).start()
+
+    steps = [(half - 2.8, 0, send_opposite, ()), (half - 1.95, 0, gates, ())]
     for g in range(groups):
         late = 0 if 2 * g < groups else 1.5
         steps.append((late, g, arrive, (g,)))
@@ -221,71 +281,14 @@
     for b in range(blocks):
         last = ((b + 1) * LANES - 1) // grows
         late = 0 if 2 * last < groups else 1.5
-        steps.append((late + half - 0.9, b, begin_sums, (b,)))
+        base = late + half - 0.9
+        steps.append((base, b, begin_sums, (b,)))
+        for step in range(2, half + 1):
+            steps.append((10 + step, b, sums, (step, b)))
+        steps.append((20, b, finish, (b,)))
+        steps.append((30, b, close, (b,)))
     for _, _, action, given in sorted(steps, key=lambda entry: entry[:2]):
         action(*given)
-
-    loads[2].wait()
-    router = dot(wr[...], tok[...], NT)
-    picked = jnp.sum(router * (iota((es, toks), 0) == ids_ref[...]).astype(F32), axis=0, keepdims=True)
-    gate_row[...] = jnp.broadcast_to(jax.nn.sigmoid(picked), gate_row.shape)
-
-    for step in range(2, half + 1):
-        for b in range(blocks):
-            for way in range(2):
-                hops = rs_hops(b)[way]
-                if step > hops:
-                    continue
-                own = partial(b, toward(way, hops - step + 1))
-                scatter(way, step - 1, b).wait_recv()
-                rs_out[way, step - 1, b] = (own + rs_in[way, step - 2, b].astype(F32)).astype(BF16)
-                scatter(way, step, b).start()
-
-    def across(k, b):
-        return pltpu.make_async_remote_copy(
-            src_ref=z_out.at[b, (zl + k) % zs], dst_ref=z_in.at[b, k - 1],
-            send_sem=z_send.at[k - 1, b], recv_sem=z_recv.at[k - 1, b],
-            device_id={"dp": ((zl + k) % zs) * ring + x}, device_id_type=MESH,
-        )
-
-    for b in range(blocks):
-        total = partial(b, x)
-        for way in range(2):
-            hops = rs_hops(b)[way]
-            scatter(way, hops, b).wait_recv()
-            total = total + rs_in[way, hops - 1, b].astype(F32)
-        total = total.reshape(zs, cols, LANES)
-        z_out[b] = total.astype(BF16)
-        for k in range(1, zs):
-            across(k, b).start()
-        z_own[b] = total
-
-    def give_back(k):
-        return pltpu.make_async_remote_copy(
-            src_ref=r_out.at[k], dst_ref=r_in.at[k], send_sem=b_send, recv_sem=b_recv,
-            device_id={"expert": me ^ k}, device_id_type=MESH,
-        )
-
-    fin[...] = jnp.zeros_like(fin)
-    first = 0
-    for b in range(blocks):
-        total = z_own[b, zl]
-        for k in range(1, zs):
-            across(k, b).wait_recv()
-            total = total + z_in[b, k - 1].astype(F32)
-        fin[b, 0:cols] = total.astype(BF16)
-        last = (b + 1) * LANES // CAP
-        back = jnp.zeros(((last - first) * PAD, 128), F32)
-        for c in range(first * CAP // LANES, b + 1):
-            part = pick[first * PAD:last * PAD, c * LANES:(c + 1) * LANES]
-            back = back + dot(part, fin[c], NT)
-        r_out[first:last] = back.astype(BF16).reshape(last - first, PAD, 128)
-
-        @pl.loop(max(first, 1), last)
-        def _(k):
-            give_back(k).start()
-
-        first = last
 
     r_in[0] = r_out[0]
     for which in range(2):
@@ -305,7 +308,7 @@
     every = pl.ds(1, es - 1)
     pltpu.make_async_copy(r_in.at[every], r_in.at[every], b_recv).wait()
     back = r_in[...].reshape(slots, 128)
-    found = lax.dot_general(placed[...], back, (((0,), (0,)), ((), ())), preferred_element_type=F32)
+    found = dot(placed_t[...], back)
     out_ref[...] = (gate_row[0:1] * found.T[:cols]).astype(BF16)
     pltpu.make_async_copy(r_out.at[every], r_out.at[every], b_send).wait()
 
@@ -353,6 +356,7 @@
             pltpu.VMEM((es, PAD, 128), BF16),
             pltpu.VMEM((8, toks), F32),
             pltpu.VMEM((es * PAD, toks), BF16),
+            pltpu.VMEM((toks, es * PAD), BF16),
             pltpu.VMEM((es * PAD, rows), BF16),
             dma((7,)),
             dma((2, groups)), dma((2, groups)),

time: 82.5 us -> 89.2 us (1.081); the launches traced: 82.3 us -> 87.9 us
  Pallas kernels: 81 us -> 86.6 us
    pallas_call x1, Pallas kernels: 81 us -> 86.6 us  [per_device(): pl.pallas_call(functools.partial(kernel, ring, zs, es), out_shape=jax.Sha...]
where the time goes in v3:
time: 89.2 us; the launch traced here: 87.9 us
  Pallas kernels  86.6 us (97%)
  local copies, waits for them, and re-layouts  1.32 us (1%)
    pallas_call x1, Pallas kernels, per_device(): pl.pallas_call(functools.partial(kernel, ring, zs, es), out_shape=jax.Sha...  86.6 us

profile of v3, /device:TPU:1, one launch (start us, length us, event | category | flops | bytes accessed | tf_op | source)
XLA Modules:
  0.0 87.9 jit_solution(13539899761535125769)
XLA Ops:
  0.0 86.6 %shard_map.64 = bf16[64,128]{1,0:T(8,128)(2,1)} custom-call(s32[1,128]{1,0:T(1,128)} %bitcast.11, bf16[128,2048]{1,0:T(8,128)(2,1)} %tok_hbm.1, bf16[32,2048]{1,0:T(8,128)(2,1)} %bitcast.10, bf16[2048,256]{1,0:T(8,128)(2,1)} %bitcast.7, bf16[2048,256]{1,0:T(8,128)(2,1)} %bitcast.8, bf16[256,2048]{1,0:T(8,128)(2,1)} %bitcast.9), custom_call_target="tpu_custom_call" | custom-call | flops 1207959552 | bytes 3145728 | tf_op jit(solution)/shard_map/pallas_call | solution.py:329
  86.6 1.3 %copy.8 = bf16[128,64]{0,1:T(8,128)(2,1)} copy(bf16[128,64]{0,1:T(8,128)(2,1)} %bitcast.6) | data formatting | bytes 32768
